TPU v7x, 256 devices: a whole 4x4x8 slice. The times are simulated.
256 devices in a mesh: dp: 32 (over x, y, core), seq: 8 (over z).
Axes of the slice: x: 4, y: 4, z: 8, core: 2. Of those that a mesh axis runs over, the one named last changes fastest.
Arguments:
- history: bfloat16 [262144, 1024], P(('dp', 'seq')), may hold values from -6 to 6
- hist_dest: int32 [262144, 1], P(('dp', 'seq')), may hold values from 0 to 31; in each aligned block of 1024 rows (0 to 1023, 1024 to 2047, ...) at most 64 rows name the same one
- hist_user: int32 [262144], P(('dp', 'seq')), may hold values from 0 to 15
- candidates: bfloat16 [8192, 1024], P(('dp', 'seq')), may hold values from -6 to 6
- cand_user: int32 [8192], P('dp'), may hold values from 0 to 15
- w_qu: bfloat16 [1024, 2048], replicated, may hold values from -0.1875 to 0.1875
- w_kv: bfloat16 [1024, 2048], replicated, may hold values from -0.1875 to 0.1875
- w_out: bfloat16 [1024, 1024], replicated, may hold values from -0.1875 to 0.1875
Outputs:
- scored: float32 [8192, 1024], P(('dp', 'seq'))
Inputs may be any that keep to these rules, and one draw needn't show every extreme that they name: `hist_dest`: among the rows of one device, no dp group is named more than 64 times; in some devices one group is named exactly 64 times.
All inputs are finite; a program needn't handle non-finite values.
Results may differ from a plain program's by a relative error of at most 0.003.
Values may be sent and summed in bfloat16 or wider, within the bound.
A program may use at most 128 MiB of HBM per device.

v0:
```python
import jax
import jax.numpy as jnp
from jax import lax
from jax.sharding import PartitionSpec as P

D = 1024
HEAD_TOTAL = 8


def silu_rows(states, weight):
    return jax.nn.silu(jnp.dot(states, weight, preferred_element_type=jnp.float32)).astype(
        jnp.bfloat16
    )


def attend(query_matrix, query_users, pair_rows, slot_users):
    count = query_matrix.shape[0]
    slots = pair_rows.shape[0]
    head_width = D // HEAD_TOTAL
    scale = head_width ** (-0.5)
    block = min(512, slots)
    query_head_rows = query_matrix.reshape(count, HEAD_TOTAL, head_width)
    pair_blocks = pair_rows.reshape(slots // block, block, 2 * D)
    user_blocks = slot_users.reshape(slots // block, block)

    def step(total_count, blocks):
        pair_block, users = blocks
        key_rows = pair_block[:, :D].reshape(block, HEAD_TOTAL, head_width)
        value_rows = pair_block[:, D:].reshape(block, HEAD_TOTAL, head_width)
        score_matrix = jnp.einsum(
            "ceu,leu->ecl", query_head_rows, key_rows, preferred_element_type=jnp.float32
        )
        visible = (query_users[:, None] == users[None, :]).astype(jnp.float32)
        weight_matrix = (jax.nn.silu(score_matrix * scale) * visible[None]).astype(jnp.bfloat16)
        return (
            total_count
            + jnp.einsum(
                "ucx,xuy->cuy", weight_matrix, value_rows, preferred_element_type=jnp.float32
            ),
            None,
        )

    start_total = jnp.zeros((count, HEAD_TOTAL, head_width), jnp.float32)
    total_count, unused = lax.scan(step, start_total, (pair_blocks, user_blocks))
    return total_count.reshape(count, D)


def on_device(history, hist_dest, hist_user, candidates, cand_user, w_qu, w_kv, w_out):
    groups = lax.axis_size("dp")
    rows = history.shape[0]
    capacity = 2 * rows // groups
    dest = hist_dest[:, 0]
    member = (dest[:, None] == jnp.arange(groups, dtype=jnp.int32)[None, :]).astype(jnp.int32)
    rank = jnp.sum((jnp.cumsum(member, axis=0) - 1) * member, axis=1)
    slot = dest * capacity + rank
    user_tags = (
        jnp.full((groups * capacity,), -1.0, jnp.bfloat16)
        .at[slot]
        .set(hist_user.astype(jnp.bfloat16))
    )
    projected = silu_rows(history, w_kv)
    send_pairs = jnp.zeros((groups * capacity, 2 * D), jnp.bfloat16).at[slot].set(projected)
    pair_rows, arrived_tags = (
        lax.all_to_all(send_pairs, "dp", split_axis=0, concat_axis=0, tiled=True),
        lax.all_to_all(user_tags, "dp", split_axis=0, concat_axis=0, tiled=True),
    )
    slot_users = arrived_tags.astype(jnp.int32)
    own_states = silu_rows(candidates, w_qu)
    query_matrix = lax.all_gather(own_states[:, :D], "seq", axis=0, tiled=True)
    gate_own = own_states[:, D:]
    attended_values = lax.psum_scatter(
        attend(query_matrix, cand_user, pair_rows, slot_users),
        "seq",
        scatter_dimension=0,
        tiled=True,
    )
    mean = jnp.mean(attended_values, axis=1, keepdims=True)
    centered = attended_values - mean
    variance = jnp.mean(centered * centered, axis=1, keepdims=True)
    normed = centered * lax.rsqrt(variance + 1e-06)
    gated = (normed * gate_own.astype(jnp.float32)).astype(jnp.bfloat16)
    mixed = candidates.astype(jnp.float32) + jnp.dot(
        gated, w_out, preferred_element_type=jnp.float32
    )
    return mixed


def solution(mesh):
    placed = (
        P(("dp", "seq"), None),
        P(("dp", "seq"), None),
        P(("dp", "seq")),
        P(("dp", "seq"), None),
        P("dp"),
        P(),
        P(),
        P(),
    )
    return jax.shard_map(
        on_device, mesh=mesh, in_specs=placed, out_specs=P(("dp", "seq"), None), check_vma=False
    )
```

profile of v0, /device:TPU:1, one launch (start us, length us, event | category | flops | bytes accessed | tf_op | source)
XLA Modules:
  0.0 301.8 jit_solution(14079728991416622969)
XLA Ops:
  6.5 0.0 copy-start
  6.5 0.8 fusion.15
  7.4 9.0 %reduce-window.6 = s32[32,8,128]{2,1,0:T(8,128)S(1)} reduce-window(s32[32,8,128]{2,1,0:T(8,128)S(1)} %fusion.15, s32[]{:T(128)} %constant.19.clone.1), window={size=1x1x128 pad=0_0x0_0x127_0}, to_apply=%region_0.0 | reduce-window | flops 4161536 | bytes 262148 | tf_op jit(solution)/shard_map/reduce-window
  16.4 0.1 slice.26
  16.5 0.1 copy.28
  16.7 0.1 copy.29
  16.7 0.1 add_add_fusion
  16.9 0.7 fusion.14
  17.6 0.7 compare_select_fusion
  18.3 0.7 convert_element_type.44
  19.0 7.6 %scatter_custom_fusion.1 = bf16[2048]{0:T(1024)(128)(2,1)S(1)} fusion(s32[1024]{0:T(1024)S(1)} %bitcast.92, bf16[1024]{0:T(1024)(128)(2,1)S(1)} %convert_element_type.44, bf16[]{:T(256)} %constant.43.clone.1), kind=kCustom, calls=%fused_computation.38 | custom fusion | bytes 4098 | tf_op jit(solution)/shard_map/scatter | solution.py:59
  26.6 0.7 all_to_all.16
  27.3 8.6 %all-to-all-start.1 = ((bf16[32,64,1]{1,2,0:T(2,128)(2,1)}), bf16[32,64,1]{1,2,0:T(2,128)(2,1)S(1)}, u32[]{:S(2)}, u32[]{:S(2)}) async-start(bf16[32,64,1]{1,2,0:T(2,128)(2,1)} %all_to_all.16), calls=%async_computation.1 | async-start | bytes 32768 | tf_op jit(solution)/shard_map/all_to_all | solution.py:65
  35.9 0.0 copy-done
  35.9 8.9 %fusion.22 = f32[1024,2048]{1,0:T(8,128)} fusion(bf16[1024,1024]{1,0:T(8,128)(2,1)S(1)} %copy-done, bf16[1024,2048]{1,0:T(8,128)(2,1)} %param.16), kind=kOutput, calls=%fused_computation.43 | convolution fusion | flops 4294967296 | bytes 14680064 | tf_op jit(solution)/shard_map/dot_general | solution.py:11
  44.7 14.5 %scatter_custom_fusion = bf16[2048,2048]{1,0:T(8,128)(2,1)} fusion(s32[1024]{0:T(1024)S(1)} %bitcast.93, f32[1024,2048]{1,0:T(8,128)} %fusion.22, f32[]{:T(128)} %constant.42.clone.1, bf16[]{:T(256)} %constant.23.clone.1), kind=kCustom, calls=%fused_computation.18 | custom fusion | flops 10485760 | bytes 16777222 | tf_op jit(solution)/shard_map/scatter | solution.py:62
  59.2 0.0 all-to-all-done.1
  59.2 0.0 copy-start.1
  59.2 7.6 %all-to-all-start = ((bf16[32,64,2048]{2,1,0:T(8,128)(2,1)}), bf16[32,64,2048]{2,1,0:T(8,128)(2,1)}, u32[]{:S(2)}, u32[]{:S(2)}) async-start(bf16[32,64,2048]{2,1,0:T(8,128)(2,1)} %bitcast.82), calls=%async_computation | async-start | bytes 16777216 | tf_op jit(solution)/shard_map/all_to_all | solution.py:64
  66.8 0.0 copy-start.2
  66.8 0.0 reduce-scatter.2.cloned.1.call-start
  66.9 0.0 copy-done.1
  66.9 3.0 %multiply_convert_fusion.2 = bf16[32,2048]{1,0:T(8,128)(2,1)S(1)} fusion(bf16[32,1024]{1,0:T(8,128)(2,1)S(1)} %copy-done.1, bf16[1024,2048]{1,0:T(8,128)(2,1)} %param.15), kind=kOutput, calls=%fused_computation.23 | convolution fusion | flops 134545408 | bytes 4390912 | tf_op jit(solution)/shard_map/dot_general | solution.py:11
  69.9 25.9 %all_gather.3 = bf16[256,1024]{1,0:T(8,128)(2,1)S(1)} all-gather(bf16[32,1024]{1,0:T(8,128)(2,1)S(1)} %slice.28), channel_id=1, replica_groups=mesh['dp'=32,'seq'=8] {'seq'}, dimensions={0}, use_global_device_ids=true | all-gather | bytes 589824 | tf_op jit(solution)/shard_map/all_gather | solution.py:69
  95.9 0.9 copy_bitcast_fusion
  96.8 0.1 convert_reduce_fusion
  96.8 0.1 reshape.88
  96.9 78.4 %all-to-all-done = bf16[32,64,2048]{2,1,0:T(8,128)(2,1)} async-done(((bf16[32,64,2048]{2,1,0:T(8,128)(2,1)}), bf16[32,64,2048]{2,1,0:T(8,128)(2,1)}, u32[]{:S(2)}, u32[]{:S(2)}) %all-to-all-start) | async-done | bytes 8388640 | tf_op jit(solution)/shard_map/all_to_all | solution.py:64
  175.3 0.0 copy-done.2
  175.3 61.5 %while.11 = (s32[]{:T(128)}, f32[256,8,128]{0,2,1:T(8,128)}, bf16[4,512,2048]{2,1,0:T(8,128)(2,1)}, bf16[256,8,128]{2,0,1:T(8,128)(2,1)}, s32[256]{0:T(256)S(1)}...) while((s32[]{:T(128)}, f32[256,8,128]{0,2,1:T(8,128)}, bf16[4,512,2048]{2,1,0:T(8,128)(2,1)}, ...), condition=%wide.region_6.7_spmd.clone, body=%wide.region_5.6_spmd.clone.sunk | while | flops 544997376 | bytes 18357352 | solution.py:44
  175.3 3.1 %constant_dynamic-slice_fusion.4 = bf16[1,512,2048]{2,1,0:T(8,128)(2,1)} fusion(bf16[4,512,2048]{2,1,0:T(8,128)(2,1)} %get-tuple-element.156, s32[]{:T(128)} %get-tuple-element.146), kind=kLoop, calls=%fused_computation.14.clone.1 | loop fusion | bytes 4194308 | tf_op jit(solution)/shard_map/while/body/jit(dynamic_index_in_dim)/dynamic_slice | solution.py:44
  178.5 3.9 %copy.43 = bf16[1,512,2048]{1,2,0:T(8,128)(2,1)} copy(bf16[1,512,2048]{2,1,0:T(8,128)(2,1)} %constant_dynamic-slice_fusion.4) | data formatting | bytes 4194304 | tf_op jit(solution)/shard_map/while/body/jit(dynamic_index_in_dim)/dynamic_slice | solution.py:44
  182.4 2.7 fusion.40
  185.1 1.0 compare_convert_fusion.2
  186.0 4.4 %fusion.41 = f32[256,8,128]{0,2,1:T(8,128)} fusion(bf16[512,8,128]{0,2,1:T(8,128)(2,1)} %bitcast.84, bf16[512,8,128]{0,2,1:T(8,128)(2,1)S(1)} %bitcast.83, bf16[256,8,128]{2,0,1:T(8,128)(2,1)} %get-tuple-element.157, f32[256,512]{0,1:T(8,128)} %compare_convert_fusion.2, f32[256,8,128]{0,2,1:T(8,128)} %get-tuple-element.147, pred[]{:T(512)S(6)} %compare.3), kind=kOutput, calls=%fused_computation.11.clone.1 | convolution fusion | flops 544735232 | bytes 5242881 | tf_op jit(solution)/shard_map/while/body/eval_jaxpr/ucx,xuy->cuy/dot_general | solution.py:37
  190.5 3.1 %constant_dynamic-slice_fusion.4 = bf16[1,512,2048]{2,1,0:T(8,128)(2,1)} fusion(bf16[4,512,2048]{2,1,0:T(8,128)(2,1)} %get-tuple-element.156, s32[]{:T(128)} %get-tuple-element.146), kind=kLoop, calls=%fused_computation.14.clone.1 | loop fusion | bytes 4194308 | tf_op jit(solution)/shard_map/while/body/jit(dynamic_index_in_dim)/dynamic_slice | solution.py:44
  193.6 3.9 %copy.43 = bf16[1,512,2048]{1,2,0:T(8,128)(2,1)} copy(bf16[1,512,2048]{2,1,0:T(8,128)(2,1)} %constant_dynamic-slice_fusion.4) | data formatting | bytes 4194304 | tf_op jit(solution)/shard_map/while/body/jit(dynamic_index_in_dim)/dynamic_slice | solution.py:44
  197.5 2.7 fusion.40
  200.2 1.0 compare_convert_fusion.2
  201.1 4.8 %fusion.41 = f32[256,8,128]{0,2,1:T(8,128)} fusion(bf16[512,8,128]{0,2,1:T(8,128)(2,1)} %bitcast.84, bf16[512,8,128]{0,2,1:T(8,128)(2,1)S(1)} %bitcast.83, bf16[256,8,128]{2,0,1:T(8,128)(2,1)} %get-tuple-element.157, f32[256,512]{0,1:T(8,128)} %compare_convert_fusion.2, f32[256,8,128]{0,2,1:T(8,128)} %get-tuple-element.147, pred[]{:T(512)S(6)} %compare.3), kind=kOutput, calls=%fused_computation.11.clone.1 | convolution fusion | flops 544735232 | bytes 5242881 | tf_op jit(solution)/shard_map/while/body/eval_jaxpr/ucx,xuy->cuy/dot_general | solution.py:37
  205.9 3.1 %constant_dynamic-slice_fusion.4 = bf16[1,512,2048]{2,1,0:T(8,128)(2,1)} fusion(bf16[4,512,2048]{2,1,0:T(8,128)(2,1)} %get-tuple-element.156, s32[]{:T(128)} %get-tuple-element.146), kind=kLoop, calls=%fused_computation.14.clone.1 | loop fusion | bytes 4194308 | tf_op jit(solution)/shard_map/while/body/jit(dynamic_index_in_dim)/dynamic_slice | solution.py:44
  209.0 3.9 %copy.43 = bf16[1,512,2048]{1,2,0:T(8,128)(2,1)} copy(bf16[1,512,2048]{2,1,0:T(8,128)(2,1)} %constant_dynamic-slice_fusion.4) | data formatting | bytes 4194304 | tf_op jit(solution)/shard_map/while/body/jit(dynamic_index_in_dim)/dynamic_slice | solution.py:44
  212.9 2.7 fusion.40
  215.6 1.0 compare_convert_fusion.2
  216.6 4.8 %fusion.41 = f32[256,8,128]{0,2,1:T(8,128)} fusion(bf16[512,8,128]{0,2,1:T(8,128)(2,1)} %bitcast.84, bf16[512,8,128]{0,2,1:T(8,128)(2,1)S(1)} %bitcast.83, bf16[256,8,128]{2,0,1:T(8,128)(2,1)} %get-tuple-element.157, f32[256,512]{0,1:T(8,128)} %compare_convert_fusion.2, f32[256,8,128]{0,2,1:T(8,128)} %get-tuple-element.147, pred[]{:T(512)S(6)} %compare.3), kind=kOutput, calls=%fused_computation.11.clone.1 | convolution fusion | flops 544735232 | bytes 5242881 | tf_op jit(solution)/shard_map/while/body/eval_jaxpr/ucx,xuy->cuy/dot_general | solution.py:37
  221.4 3.1 %constant_dynamic-slice_fusion.4 = bf16[1,512,2048]{2,1,0:T(8,128)(2,1)} fusion(bf16[4,512,2048]{2,1,0:T(8,128)(2,1)} %get-tuple-element.156, s32[]{:T(128)} %get-tuple-element.146), kind=kLoop, calls=%fused_computation.14.clone.1 | loop fusion | bytes 4194308 | tf_op jit(solution)/shard_map/while/body/jit(dynamic_index_in_dim)/dynamic_slice | solution.py:44
  224.5 3.9 %copy.43 = bf16[1,512,2048]{1,2,0:T(8,128)(2,1)} copy(bf16[1,512,2048]{2,1,0:T(8,128)(2,1)} %constant_dynamic-slice_fusion.4) | data formatting | bytes 4194304 | tf_op jit(solution)/shard_map/while/body/jit(dynamic_index_in_dim)/dynamic_slice | solution.py:44
  228.4 2.7 fusion.40
  231.1 1.0 compare_convert_fusion.2
  232.0 4.8 %fusion.41 = f32[256,8,128]{0,2,1:T(8,128)} fusion(bf16[512,8,128]{0,2,1:T(8,128)(2,1)} %bitcast.84, bf16[512,8,128]{0,2,1:T(8,128)(2,1)S(1)} %bitcast.83, bf16[256,8,128]{2,0,1:T(8,128)(2,1)} %get-tuple-element.157, f32[256,512]{0,1:T(8,128)} %compare_convert_fusion.2, f32[256,8,128]{0,2,1:T(8,128)} %get-tuple-element.147, pred[]{:T(512)S(6)} %compare.3), kind=kOutput, calls=%fused_computation.11.clone.1 | convolution fusion | flops 544735232 | bytes 5242881 | tf_op jit(solution)/shard_map/while/body/eval_jaxpr/ucx,xuy->cuy/dot_general | solution.py:37
  236.8 2.5 copy.36
  239.4 0.0 reduce-scatter.2.cloned.1.call-update
  239.4 50.6 %reduce-scatter.2.cloned.1.call-done = f32[32,1024]{1,0:T(8,128)} async-done(((f32[256,1024]{1,0:T(8,128)}), f32[32,1024]{1,0:T(8,128)}) %reduce-scatter.2.cloned.1.call-update) | async-done | bytes 131088 | tf_op jit(solution)/shard_map/reduce_scatter | solution.py:71
  289.9 1.0 reduce_sum.31
  291.0 1.1 multiply_reduce_fusion
  292.1 2.9 convolution_add_fusion
  (10 shorter events, 0.1 us)
Async XLA Ops:
  6.5 29.3 %copy-start = (bf16[1024,1024]{1,0:T(8,128)(2,1)S(1)}, bf16[1024,1024]{1,0:T(8,128)(2,1)}, u32[]{:S(2)}) copy-start(bf16[1024,1024]{1,0:T(8,128)(2,1)} %param.10) | copy-start | bytes 6291460
  27.3 32.0 %all-to-all-start.1 = ((bf16[32,64,1]{1,2,0:T(2,128)(2,1)}), bf16[32,64,1]{1,2,0:T(2,128)(2,1)S(1)}, u32[]{:S(2)}, u32[]{:S(2)}) async-start(bf16[32,64,1]{1,2,0:T(2,128)(2,1)} %all_to_all.16), calls=%async_computation.1 | async-start | bytes 32768 | tf_op jit(solution)/shard_map/all_to_all | solution.py:65
  59.2 7.7 %copy-start.1 = (bf16[32,1024]{1,0:T(8,128)(2,1)S(1)}, bf16[32,1024]{1,0:T(8,128)(2,1)}, u32[]{:S(2)}) copy-start(bf16[32,1024]{1,0:T(8,128)(2,1)} %param.13) | copy-start | bytes 196612
  59.2 116.1 %all-to-all-start = ((bf16[32,64,2048]{2,1,0:T(8,128)(2,1)}), bf16[32,64,2048]{2,1,0:T(8,128)(2,1)}, u32[]{:S(2)}, u32[]{:S(2)}) async-start(bf16[32,64,2048]{2,1,0:T(8,128)(2,1)} %bitcast.82), calls=%async_computation | async-start | bytes 16777216 | tf_op jit(solution)/shard_map/all_to_all | solution.py:64
  66.8 108.5 %copy-start.2 = (s32[256]{0:T(256)S(1)}, s32[256]{0:T(256)}, u32[]{:S(2)}) copy-start(s32[256]{0:T(256)} %param.14) | copy-start | bytes 3076
  66.8 223.1 %reduce-scatter.2.cloned.1.call-start = ((), (), s32[]{:S(2)}) async-start(), calls=%async_computation.3 | async-start | bytes 1179648 | tf_op jit(solution)/shard_map/reduce_scatter | solution.py:71
Sparse Core Ops, SparseCore 0:
  239.5 50.3 reduce-scatter.1
where the time goes:
time: 307 us; the launch traced here: 302 us
  waiting for transfers between devices  129 us (42%)
  local copies, waits for them, and re-layouts  50.9 us (17%)
  matrix products  33.4 us (11%)
  other arithmetic  32.7 us (11%)
  blocking collectives  25.9 us (8%)
  starting transfers between devices  16.2 us (5%)
  between operations  13.5 us (4%)
    all_to_all x1, waiting for transfers between devices, on_device(): lax.all_to_all(send_pairs, 'dp', split_axis=0, concat_axis=0, tiled=True)  78.4 us
    reduce_scatter x1, waiting for transfers between devices, on_device(): lax.psum_scatter(attend(query_matrix, cand_user, pair_rows, slot_users),...  50.6 us
    dynamic_slice x12, local copies, waits for them, and re-layouts, attend(): lax.scan(step, start_total, (pair_blocks, user_blocks))  28.2 us
    all_gather x1, blocking collectives, on_device(): query_matrix = lax.all_gather(own_states[:, :D], 'seq', axis=0, tiled=True)  25.9 us
    dot_general x4, matrix products, step(): jnp.einsum('ucx,xuy->cuy', weight_matrix, value_rows, preferred_element_t...  18.7 us
    scatter x1, other arithmetic, on_device(): jnp.zeros((groups * capacity, 2 * D), jnp.bfloat16).at[slot].set(projected)  14.5 us
    dot_general x2, matrix products, silu_rows(): jnp.dot(states, weight, preferred_element_type=jnp.float32)  11.9 us
    slice x4, local copies, waits for them, and re-layouts, step(): key_rows = pair_block[:, :D].reshape(block, HEAD_TOTAL, head_width)  10.6 us
  transfers between devices with their start and end apart: 3, of which 2 were waited for; matrix products, arithmetic and copies ran while one was open for 9% of the time, Pallas kernels for 0%

commit v1 on v0

v1 whole, which is shorter than its diff:
```python
import functools

import jax
import jax.numpy as jnp
from jax import lax
from jax.experimental import pallas as pl
from jax.experimental.pallas import tpu as pltpu
from jax.sharding import PartitionSpec as P

D = 1024
HEADS = 8
HW = D // HEADS
ROWS = 1024
GROUPS = 32
SEQ = 8
CAP = 2 * ROWS // GROUPS
CAND = 32
GROUP_CAND = CAND * SEQ
PER = 4
BATCH = PER * CAP
BATCHES = GROUPS // PER
SELF_BATCH = 2
MESH = pl.DeviceIdType.MESH
HEAD_UNROLL = 2


def silu_half(half):
    return half + half * jnp.tanh(half)


def kernel(
    history, dest_ref, user_ref, candidates, cand_user, w_qu, w_kv, w_out, out_ref,
    hist, qu_w, kv_w, out_w, send, recv, tag_send, tag_recv, slot_ref, qu, q_all, user_mat,
    mask, total, part_send, part_recv,
    load_sem, kv_sem, send_sem, recv_sem, tag_send_sem, tag_recv_sem, q_send_sem, q_recv_sem,
    part_send_sem, part_recv_sem, self_sem,
):
    dp = lax.axis_index("dp")
    z = lax.axis_index("seq")
    core = lax.rem(dp, 2)
    y = lax.rem(lax.div(dp, 2), 4)
    x = lax.div(dp, 8)
    sign = 1 - 2 * core

    load_hist = pltpu.make_async_copy(history, hist, load_sem.at[0])
    load_qu = pltpu.make_async_copy(w_qu, qu_w, load_sem.at[1])
    load_out = pltpu.make_async_copy(w_out, out_w, load_sem.at[2])
    load_hist.start()

    barrier = pltpu.get_barrier_semaphore()

    def greet(i, carry):
        @pl.when(i != dp)
        def _():
            pl.semaphore_signal(barrier, inc=1, device_id=(i, z), device_id_type=MESH)

        return carry

    lax.fori_loop(0, GROUPS, greet, 0)
    for d in range(1, SEQ):
        pl.semaphore_signal(
            barrier, inc=1, device_id=(dp, lax.rem(z + d, SEQ)), device_id_type=MESH
        )

    load_qu.start()

    def kv_copies(h):
        cols = pl.ds(pl.multiple_of(h * HW, HW), HW)
        cols_v = pl.ds(pl.multiple_of(D + h * HW, HW), HW)
        return (
            pltpu.make_async_copy(w_kv.at[:, cols], kv_w.at[h, :, pl.ds(0, HW)], kv_sem.at[2 * h]),
            pltpu.make_async_copy(
                w_kv.at[:, cols_v], kv_w.at[h, :, pl.ds(HW, HW)], kv_sem.at[2 * h + 1]
            ),
        )

    def start_kv(h, carry):
        for copy in kv_copies(h):
            copy.start()
        return carry

    lax.fori_loop(0, HEADS, start_kv, 0)
    load_out.start()

    blocks = ROWS // 128
    group_ids = lax.broadcasted_iota(jnp.int32, (GROUPS, 128), 0)
    members = [
        (dest_ref[:, b * 128 : (b + 1) * 128] == group_ids).astype(jnp.float32)
        for b in range(blocks)
    ]
    upper = (
        lax.broadcasted_iota(jnp.int32, (128, 128), 0)
        <= lax.broadcasted_iota(jnp.int32, (128, 128), 1)
    ).astype(jnp.float32)
    running = jnp.dot(
        jnp.concatenate(members, axis=0).astype(jnp.bfloat16),
        upper.astype(jnp.bfloat16),
        preferred_element_type=jnp.float32,
    )
    before = jnp.zeros((GROUPS, 1), jnp.float32)
    for b in range(blocks):
        inside = running[b * GROUPS : (b + 1) * GROUPS]
        rank = jnp.sum(members[b] * (inside + (before - 1.0)), axis=0, keepdims=True)
        slot_ref[:, b * 128 : (b + 1) * 128] = (
            dest_ref[:, b * 128 : (b + 1) * 128] * CAP + rank.astype(jnp.int32)
        )
        before = before + inside[:, 127:128]

    load_hist.wait()
    pl.semaphore_wait(barrier, GROUPS - 1 + SEQ - 1)

    def target(j, i):
        jj = lax.rem(j, 4)
        other = lax.div(j, 4)
        a = jnp.where(jj == 1, 2, 1)
        b = jnp.where(jj == 3, 0, 1)
        dx, dy = ((a, b), (-b, a), (-a, -b), (b, -a))[i]
        dx = jnp.where(jj == SELF_BATCH, 2 * (i % 2), dx)
        dy = jnp.where(jj == SELF_BATCH, 2 * (i // 2), dy)
        to_x = lax.rem(x + sign * dx + 4, 4)
        to_y = lax.rem(y + sign * dy + 4, 4)
        return to_x * 8 + to_y * 2 + lax.rem(core + other, 2)

    def row_copy(j, i):
        k = j * PER + i
        rows = pl.ds(pl.multiple_of(k * CAP, CAP), CAP)
        return pltpu.make_async_remote_copy(
            send.at[rows], recv.at[rows], send_sem.at[k], recv_sem.at[k],
            device_id=(target(j, i), z), device_id_type=MESH,
        )

    def tag_copy(j, i):
        k = j * PER + i
        return pltpu.make_async_remote_copy(
            tag_send.at[2 * j + i // 2], tag_recv.at[k], tag_send_sem.at[k], tag_recv_sem.at[k],
            device_id=(target(j, i), z), device_id_type=MESH,
        )

    self_rows = pl.ds(SELF_BATCH * PER * CAP, CAP)
    self_copy = pltpu.make_async_copy(send.at[self_rows], recv.at[self_rows], self_sem.at[0])
    self_tag = pltpu.make_async_copy(
        tag_send.at[2 * SELF_BATCH], tag_recv.at[SELF_BATCH * PER], self_sem.at[1]
    )

    users = user_ref[...].astype(jnp.float32).astype(jnp.bfloat16)
    users = jnp.broadcast_to(users, (16, ROWS))
    slot_row = slot_ref[...]

    def pack(j, carry):
        inside = lax.broadcasted_iota(jnp.int32, (CAP, ROWS), 0)
        picks = jnp.concatenate(
            [
                ((slot_row - target(j, i) * CAP) == inside).astype(jnp.float32)
                for i in range(PER)
            ],
            axis=0,
        ).astype(jnp.bfloat16)
        tags = lax.dot_general(
            users, picks, (((1,), (1,)), ((), ())), preferred_element_type=jnp.float32
        )
        tag_send[2 * j] = tags[0:1, 0:128]
        tag_send[2 * j + 1] = tags[0:1, 128:256]
        rows = pl.ds(pl.multiple_of(j * BATCH, BATCH), BATCH)
        for c in range(D // 256):
            send[rows, c * 256 : (c + 1) * 256] = jnp.dot(
                picks, hist[:, c * 256 : (c + 1) * 256], preferred_element_type=jnp.float32
            ).astype(jnp.bfloat16)
        for i in range(PER):
            if i == 0:
                @pl.when(j != SELF_BATCH)
                def _():
                    row_copy(j, 0).start()
                    tag_copy(j, 0).start()

                @pl.when(j == SELF_BATCH)
                def _():
                    self_copy.start()
                    self_tag.start()
            else:
                row_copy(j, i).start()
                tag_copy(j, i).start()
        return carry

    lax.fori_loop(0, BATCHES, pack, 0)

    load_qu.wait()

    def project_own(c, carry):
        cols = pl.ds(pl.multiple_of(c * 256, 256), 256)
        qu[:, cols] = silu_half(
            0.5 * jnp.dot(candidates[...], qu_w[:, cols], preferred_element_type=jnp.float32)
        ).astype(jnp.bfloat16)
        return carry

    lax.fori_loop(0, 2 * D // 256, project_own, 0)
    own_rows = pl.ds(pl.multiple_of(z * CAND, CAND), CAND)
    q_all[own_rows, :] = qu[:, :D]

    def q_copy(d):
        return pltpu.make_async_remote_copy(
            qu.at[:, pl.ds(0, D)], q_all.at[own_rows], q_send_sem.at[d], q_recv_sem.at[d],
            device_id=(dp, lax.rem(z + d, SEQ)), device_id_type=MESH,
        )

    for d in range(1, SEQ):
        q_copy(d).start()

    square = (
        lax.broadcasted_iota(jnp.int32, (GROUP_CAND, GROUP_CAND), 0)
        == lax.broadcasted_iota(jnp.int32, (GROUP_CAND, GROUP_CAND), 1)
    )
    cand_col = jnp.sum(
        jnp.where(square, cand_user[...].astype(jnp.float32), 0.0), axis=1, keepdims=True
    )
    user_mat[...] = jnp.broadcast_to(cand_col, (GROUP_CAND, BATCH))
    total[...] = jnp.zeros_like(total)

    def finish_kv(h, carry):
        for copy in kv_copies(h):
            copy.wait()
        return carry

    lax.fori_loop(0, HEADS, finish_kv, 0)
    for d in range(1, SEQ):
        q_copy(d).wait_recv()

    low = lax.broadcasted_iota(jnp.int32, (1, 128), 1) < CAP
    scale = 0.5 * HW ** (-0.5)

    def attend(j, carry):
        for i in range(PER):
            if i == 0:
                @pl.when(j != SELF_BATCH)
                def _():
                    row_copy(j, 0).wait_recv()
                    tag_copy(j, 0).wait_recv()

                @pl.when(j == SELF_BATCH)
                def _():
                    self_copy.wait()
                    self_tag.wait()
            else:
                row_copy(j, i).wait_recv()
                tag_copy(j, i).wait_recv()
        tags = jnp.concatenate(
            [
                jnp.where(low, tag_recv[j * PER], tag_recv[j * PER + 1]),
                jnp.where(low, tag_recv[j * PER + 2], tag_recv[j * PER + 3]),
            ],
            axis=1,
        )
        mask[...] = (user_mat[...] == tags).astype(jnp.float32)
        rows = pl.ds(pl.multiple_of(j * BATCH, BATCH), BATCH)

        def heads(step, carry):
            for sub in range(HEAD_UNROLL):
                h = step * HEAD_UNROLL + sub
                kv = silu_half(
                    0.5 * jnp.dot(recv[rows, :], kv_w[h], preferred_element_type=jnp.float32)
                ).astype(jnp.bfloat16)
                q_head = q_all[:, pl.ds(pl.multiple_of(h * HW, HW), HW)]
                half = scale * lax.dot_general(
                    q_head, kv[:, :HW], (((1,), (1,)), ((), ())),
                    preferred_element_type=jnp.float32,
                )
                weight = (silu_half(half) * mask[...]).astype(jnp.bfloat16)
                total[h] += jnp.dot(weight, kv[:, HW:], preferred_element_type=jnp.float32)
            return carry

        return lax.fori_loop(0, HEADS // HEAD_UNROLL, heads, carry)

    lax.fori_loop(0, BATCHES, attend, 0)

    for h in range(HEADS):
        part_send[:, h * HW : (h + 1) * HW] = total[h].astype(jnp.bfloat16)

    def part_copy(d):
        peer = lax.rem(z + d, SEQ)
        return pltpu.make_async_remote_copy(
            part_send.at[pl.ds(pl.multiple_of(peer * CAND, CAND), CAND)],
            part_recv.at[d], part_send_sem.at[d], part_recv_sem.at[d],
            device_id=(dp, peer), device_id_type=MESH,
        )

    for d in (4, 3, 5, 2, 6, 1, 7):
        part_copy(d).start()
    load_out.wait()
    attended = jnp.concatenate([total[h, own_rows, :] for h in range(HEADS)], axis=1)
    for d in (1, 7, 2, 6, 3, 5, 4):
        part_copy(d).wait_recv()
        attended = attended + part_recv[d].astype(jnp.float32)
    mean = jnp.mean(attended, axis=1, keepdims=True)
    centered = attended - mean
    variance = jnp.mean(centered * centered, axis=1, keepdims=True)
    normed = centered * lax.rsqrt(variance + 1e-06)
    gated = (normed * qu[:, D:].astype(jnp.float32)).astype(jnp.bfloat16)
    for c in range(D // 256):
        cols = slice(c * 256, (c + 1) * 256)
        out_ref[:, cols] = candidates[:, cols].astype(jnp.float32) + jnp.dot(
            gated, out_w[:, cols], preferred_element_type=jnp.float32
        )

    def drain(j, carry):
        for i in range(PER):
            if i == 0:
                @pl.when(j != SELF_BATCH)
                def _():
                    row_copy(j, 0).wait_send()
                    tag_copy(j, 0).wait_send()
            else:
                row_copy(j, i).wait_send()
                tag_copy(j, i).wait_send()
        return carry

    lax.fori_loop(0, BATCHES, drain, 0)
    for d in range(1, SEQ):
        q_copy(d).wait_send()
        part_copy(d).wait_send()


def on_device(history, hist_dest, hist_user, candidates, cand_user, w_qu, w_kv, w_out):
    vmem = pl.BlockSpec(memory_space=pltpu.VMEM)
    hbm = pl.BlockSpec(memory_space=pl.ANY)
    dma = pltpu.SemaphoreType.DMA
    bf16, f32 = jnp.bfloat16, jnp.float32
    return pl.pallas_call(
        kernel,
        out_shape=jax.ShapeDtypeStruct((CAND, D), f32),
        in_specs=[hbm, vmem, vmem, vmem, vmem, hbm, hbm, hbm],
        out_specs=vmem,
        scratch_shapes=[
            pltpu.VMEM((ROWS, D), bf16),
            pltpu.VMEM((D, 2 * D), bf16),
            pltpu.VMEM((HEADS, D, 2 * HW), bf16),
            pltpu.VMEM((D, D), bf16),
            pltpu.VMEM((GROUPS * CAP, D), bf16),
            pltpu.VMEM((GROUPS * CAP, D), bf16),
            pltpu.VMEM((2 * BATCHES, 1, 128), f32),
            pltpu.VMEM((GROUPS, 1, 128), f32),
            pltpu.VMEM((1, ROWS), jnp.int32),
            pltpu.VMEM((CAND, 2 * D), bf16),
            pltpu.VMEM((GROUP_CAND, D), bf16),
            pltpu.VMEM((GROUP_CAND, BATCH), f32),
            pltpu.VMEM((GROUP_CAND, BATCH), f32),
            pltpu.VMEM((HEADS, GROUP_CAND, HW), f32),
            pltpu.VMEM((GROUP_CAND, D), bf16),
            pltpu.VMEM((SEQ, CAND, D), bf16),
            dma((3,)),
            dma((2 * HEADS,)),
            dma((GROUPS,)),
            dma((GROUPS,)),
            dma((GROUPS,)),
            dma((GROUPS,)),
            dma((SEQ,)),
            dma((SEQ,)),
            dma((SEQ,)),
            dma((SEQ,)),
            dma((2,)),
        ],
        compiler_params=pltpu.CompilerParams(
            collective_id=0, has_side_effects=True, vmem_limit_bytes=56 << 20
        ),
        name="route_attend_score",
    )(
        history, hist_dest.reshape(1, ROWS), hist_user.reshape(1, ROWS), candidates,
        cand_user.reshape(1, GROUP_CAND), w_qu, w_kv, w_out,
    )


def solution(mesh):
    placed = (
        P(("dp", "seq"), None),
        P(("dp", "seq"), None),
        P(("dp", "seq")),
        P(("dp", "seq"), None),
        P("dp"),
        P(),
        P(),
        P(),
    )
    return jax.shard_map(
        on_device, mesh=mesh, in_specs=placed, out_specs=P(("dp", "seq"), None), check_vma=False
    )
```

time: 307 us -> 94.6 us (0.31); the launches traced: 302 us -> 94.4 us
  waiting for transfers between devices: 129 us -> 0 us
  Pallas kernels: 0 us -> 92.9 us
  local copies, waits for them, and re-layouts: 50.9 us -> 1.57 us
  matrix products: 33.4 us -> 0 us
  other arithmetic: 32.7 us -> 0 us
  blocking collectives: 25.9 us -> 0 us
  starting transfers between devices: 16.2 us -> 0 us
  between operations: 13.5 us -> 0.01 us
    pallas_call x0 -> x1, Pallas kernels: none -> 92.9 us  [on_device(): pl.pallas_call(kernel, out_shape=jax.ShapeDtypeStruct((CAND, D), f32), in...]
    all_to_all x2 -> x0, waiting for transfers between devices: 78.4 us -> none  [the longest x1 78.4 us: on_device(): lax.all_to_all(send_pairs, 'dp', split_axis=0, concat_axis=0, tiled=True)]
    reduce_scatter x1 -> x0, waiting for transfers between devices: 50.6 us -> none  [on_device(): lax.psum_scatter(attend(query_matrix, cand_user, pair_rows, slot_users),...]
    dot_general x7 -> x0, matrix products: 33.4 us -> none  [the longest x4 18.7 us: step(): jnp.einsum('ucx,xuy->cuy', weight_matrix, value_rows, preferred_element_t...]
    dynamic_slice x12 -> x0, local copies, waits for them, and re-layouts: 28.2 us -> none  [attend(): lax.scan(step, start_total, (pair_blocks, user_blocks))]
    all_gather x1 -> x0, blocking collectives: 25.9 us -> none  [on_device(): query_matrix = lax.all_gather(own_states[:, :D], 'seq', axis=0, tiled=True)]
    all_to_all x2 -> x0, starting transfers between devices: 16.2 us -> none  [the longest x1 8.6 us: on_device(): lax.all_to_all(user_tags, 'dp', split_axis=0, concat_axis=0, tiled=True)]
    scatter x1 -> x0, other arithmetic: 14.5 us -> none  [on_device(): jnp.zeros((groups * capacity, 2 * D), jnp.bfloat16).at[slot].set(projected)]
  transfers between devices with their start and end apart: 3 -> 0, of which waited for: 2 -> 0; matrix products, arithmetic and copies ran while one was open for 9% -> 0% of each run, Pallas kernels for 0% -> 0%
where the time goes in v1:
time: 94.6 us; the launch traced here: 94.4 us
  Pallas kernels  92.9 us (98%)
  local copies, waits for them, and re-layouts  1.57 us (2%)
    pallas_call x1, Pallas kernels, on_device(): pl.pallas_call(kernel, out_shape=jax.ShapeDtypeStruct((CAND, D), f32), in...  92.9 us

profile of v1, /device:TPU:1, one launch (start us, length us, event | category | flops | bytes accessed | tf_op | source)
XLA Modules:
  0.0 94.4 jit_solution(639090213164372163)
XLA Ops:
  0.0 92.9 %route_attend_score.1 = f32[32,1024]{1,0:T(8,128)} custom-call(bf16[1024,1024]{1,0:T(8,128)(2,1)} %history.1, s32[1,1024]{1,0:T(1,128)} %bitcast.3, s32[1,1024]{1,0:T(1,128)} %bitcast.4, bf16[32,1024]{1,0:T(8,128)(2,1)} %candidates.1, s32[1,256]{1,0:T(1,128)} %bitcast.5, bf16[1024,2048]{1,0:T(8,128)(2,1)} %w_qu.1, bf16[1024,2048]{1,0:T(8,128)(2,1)} %w_kv.1, ...), custom_call_target="tpu_custom_call" | custom-call | tf_op jit(solution)/shard_map/route_attend_score/pallas_call | solution.py:326
  92.9 1.6 %copy.10 = f32[32,1024]{1,0:T(8,128)} copy(f32[32,1024]{1,0:T(8,128)} %route_attend_score.1) | data formatting | bytes 262144

commit v2 on v1

--- a/solution.py
+++ b/solution.py
@@ -19,9 +19,9 @@
 PER = 4
 BATCH = PER * CAP
 BATCHES = GROUPS // PER
-SELF_BATCH = 2
 MESH = pl.DeviceIdType.MESH
-HEAD_UNROLL = 2
+PACKED_FIRST = 2
+SELF_PLACE = 3
 
 
 def silu_half(half):
@@ -31,7 +31,7 @@
 def kernel(
     history, dest_ref, user_ref, candidates, cand_user, w_qu, w_kv, w_out, out_ref,
     hist, qu_w, kv_w, out_w, send, recv, tag_send, tag_recv, slot_ref, qu, q_all, user_mat,
-    mask, total, part_send, part_recv,
+    mask, kv_ref, total, part_send, part_recv,
     load_sem, kv_sem, send_sem, recv_sem, tag_send_sem, tag_recv_sem, q_send_sem, q_recv_sem,
     part_send_sem, part_recv_sem, self_sem,
 ):
@@ -42,45 +42,37 @@
     x = lax.div(dp, 8)
     sign = 1 - 2 * core
 
-    load_hist = pltpu.make_async_copy(history, hist, load_sem.at[0])
-    load_qu = pltpu.make_async_copy(w_qu, qu_w, load_sem.at[1])
-    load_out = pltpu.make_async_copy(w_out, out_w, load_sem.at[2])
-    load_hist.start()
+    step = ROWS // 4
+    load_hist = [
+        pltpu.make_async_copy(
+            history.at[pl.ds(c * step, step)], hist.at[pl.ds(c * step, step)], load_sem.at[c]
+        )
+        for c in range(4)
+    ]
+    load_qu = pltpu.make_async_copy(w_qu, qu_w, load_sem.at[4])
+    load_out = pltpu.make_async_copy(w_out, out_w, load_sem.at[5])
+    for copy in load_hist:
+        copy.start()
 
     barrier = pltpu.get_barrier_semaphore()
-
-    def greet(i, carry):
-        @pl.when(i != dp)
-        def _():
-            pl.semaphore_signal(barrier, inc=1, device_id=(i, z), device_id_type=MESH)
-
-        return carry
-
-    lax.fori_loop(0, GROUPS, greet, 0)
+    for other in range(1, GROUPS):
+        pl.semaphore_signal(
+            barrier, inc=1, device_id=(lax.rem(dp + other, GROUPS), z), device_id_type=MESH
+        )
     for d in range(1, SEQ):
         pl.semaphore_signal(
             barrier, inc=1, device_id=(dp, lax.rem(z + d, SEQ)), device_id_type=MESH
         )
 
-    load_qu.start()
-
     def kv_copies(h):
-        cols = pl.ds(pl.multiple_of(h * HW, HW), HW)
-        cols_v = pl.ds(pl.multiple_of(D + h * HW, HW), HW)
+        cols = pl.ds(h * HW, HW)
+        cols_v = pl.ds(D + h * HW, HW)
         return (
             pltpu.make_async_copy(w_kv.at[:, cols], kv_w.at[h, :, pl.ds(0, HW)], kv_sem.at[2 * h]),
             pltpu.make_async_copy(
                 w_kv.at[:, cols_v], kv_w.at[h, :, pl.ds(HW, HW)], kv_sem.at[2 * h + 1]
             ),
         )
-
-    def start_kv(h, carry):
-        for copy in kv_copies(h):
-            copy.start()
-        return carry
-
-    lax.fori_loop(0, HEADS, start_kv, 0)
-    load_out.start()
 
     blocks = ROWS // 128
     group_ids = lax.broadcasted_iota(jnp.int32, (GROUPS, 128), 0)
@@ -106,47 +98,71 @@
         )
         before = before + inside[:, 127:128]
 
-    load_hist.wait()
-    pl.semaphore_wait(barrier, GROUPS - 1 + SEQ - 1)
+    for copy in load_hist:
+        copy.wait()
+    load_qu.start()
+    for h in range(HEADS):
+        for copy in kv_copies(h):
+            copy.start()
+    load_out.start()
 
     def target(j, i):
         jj = lax.rem(j, 4)
-        other = lax.div(j, 4)
-        a = jnp.where(jj == 1, 2, 1)
+        a = jnp.where(jj == 2, 2, 1)
         b = jnp.where(jj == 3, 0, 1)
         dx, dy = ((a, b), (-b, a), (-a, -b), (b, -a))[i]
-        dx = jnp.where(jj == SELF_BATCH, 2 * (i % 2), dx)
-        dy = jnp.where(jj == SELF_BATCH, 2 * (i // 2), dy)
+        dx = jnp.where(jj == 0, 2 * (1 - i % 2), dx)
+        dy = jnp.where(jj == 0, 2 * (1 - i // 2), dy)
         to_x = lax.rem(x + sign * dx + 4, 4)
         to_y = lax.rem(y + sign * dy + 4, 4)
-        return to_x * 8 + to_y * 2 + lax.rem(core + other, 2)
+        return to_x * 8 + to_y * 2 + lax.div(j, 4)
+
+    def block(k):
+        return pl.ds(pl.multiple_of(k * CAP, CAP), CAP)
 
     def row_copy(j, i):
         k = j * PER + i
-        rows = pl.ds(pl.multiple_of(k * CAP, CAP), CAP)
+        r = lax.rem(j, 4) * 2 * PER + core * PER + i
         return pltpu.make_async_remote_copy(
-            send.at[rows], recv.at[rows], send_sem.at[k], recv_sem.at[k],
+            send.at[block(k)], recv.at[block(r)], send_sem.at[k], recv_sem.at[r],
             device_id=(target(j, i), z), device_id_type=MESH,
         )
 
     def tag_copy(j, i):
         k = j * PER + i
+        r = lax.rem(j, 4) * 2 * PER + core * PER + i
         return pltpu.make_async_remote_copy(
-            tag_send.at[2 * j + i // 2], tag_recv.at[k], tag_send_sem.at[k], tag_recv_sem.at[k],
+            tag_send.at[2 * j + i // 2], tag_recv.at[r], tag_send_sem.at[k], tag_recv_sem.at[r],
             device_id=(target(j, i), z), device_id_type=MESH,
         )
 
-    self_rows = pl.ds(SELF_BATCH * PER * CAP, CAP)
-    self_copy = pltpu.make_async_copy(send.at[self_rows], recv.at[self_rows], self_sem.at[0])
+    def arrival(r):
+        return (
+            pltpu.make_async_remote_copy(
+                send.at[block(r)], recv.at[block(r)], send_sem.at[r], recv_sem.at[r],
+                device_id=(dp, lax.rem(z + 1, SEQ)), device_id_type=MESH,
+            ),
+            pltpu.make_async_remote_copy(
+                tag_send.at[0], tag_recv.at[r], tag_send_sem.at[r], tag_recv_sem.at[r],
+                device_id=(dp, lax.rem(z + 1, SEQ)), device_id_type=MESH,
+            ),
+        )
+
+    self_part = core * 4
+    self_copy = pltpu.make_async_copy(
+        send.at[block(self_part * PER + SELF_PLACE)], recv.at[block(core * PER + SELF_PLACE)],
+        self_sem.at[0],
+    )
     self_tag = pltpu.make_async_copy(
-        tag_send.at[2 * SELF_BATCH], tag_recv.at[SELF_BATCH * PER], self_sem.at[1]
+        tag_send.at[2 * self_part + SELF_PLACE // 2], tag_recv.at[core * PER + SELF_PLACE],
+        self_sem.at[1],
     )
 
     users = user_ref[...].astype(jnp.float32).astype(jnp.bfloat16)
     users = jnp.broadcast_to(users, (16, ROWS))
     slot_row = slot_ref[...]
 
-    def pack(j, carry):
+    def pack(j):
         inside = lax.broadcasted_iota(jnp.int32, (CAP, ROWS), 0)
         picks = jnp.concatenate(
             [
@@ -165,34 +181,39 @@
             send[rows, c * 256 : (c + 1) * 256] = jnp.dot(
                 picks, hist[:, c * 256 : (c + 1) * 256], preferred_element_type=jnp.float32
             ).astype(jnp.bfloat16)
+
+    def dispatch(j):
         for i in range(PER):
-            if i == 0:
-                @pl.when(j != SELF_BATCH)
+            if i == SELF_PLACE:
+                @pl.when(j != self_part)
                 def _():
-                    row_copy(j, 0).start()
-                    tag_copy(j, 0).start()
-
-                @pl.when(j == SELF_BATCH)
+                    row_copy(j, i).start()
+                    tag_copy(j, i).start()
+
+                @pl.when(j == self_part)
                 def _():
                     self_copy.start()
                     self_tag.start()
             else:
                 row_copy(j, i).start()
                 tag_copy(j, i).start()
+
+    def dispatch_and_pack(j, carry):
+        dispatch(j)
+        pack(j + 1)
         return carry
 
-    lax.fori_loop(0, BATCHES, pack, 0)
+    pack(0)
+    pl.semaphore_wait(barrier, GROUPS - 1 + SEQ - 1)
+    lax.fori_loop(0, PACKED_FIRST, dispatch_and_pack, 0)
 
     load_qu.wait()
 
-    def project_own(c, carry):
-        cols = pl.ds(pl.multiple_of(c * 256, 256), 256)
+    for c in range(2 * D // 256):
+        cols = slice(c * 256, (c + 1) * 256)
         qu[:, cols] = silu_half(
             0.5 * jnp.dot(candidates[...], qu_w[:, cols], preferred_element_type=jnp.float32)
         ).astype(jnp.bfloat16)
-        return carry
-
-    lax.fori_loop(0, 2 * D // 256, project_own, 0)
     own_rows = pl.ds(pl.multiple_of(z * CAND, CAND), CAND)
     q_all[own_rows, :] = qu[:, :D]
 
@@ -204,6 +225,8 @@
 
     for d in range(1, SEQ):
         q_copy(d).start()
+    lax.fori_loop(PACKED_FIRST, BATCHES - 1, dispatch_and_pack, 0)
+    dispatch(BATCHES - 1)
 
     square = (
         lax.broadcasted_iota(jnp.int32, (GROUP_CAND, GROUP_CAND), 0)
@@ -215,64 +238,75 @@
     user_mat[...] = jnp.broadcast_to(cand_col, (GROUP_CAND, BATCH))
     total[...] = jnp.zeros_like(total)
 
-    def finish_kv(h, carry):
+    for h in range(HEADS):
         for copy in kv_copies(h):
             copy.wait()
-        return carry
-
-    lax.fori_loop(0, HEADS, finish_kv, 0)
-    for d in range(1, SEQ):
-        q_copy(d).wait_recv()
 
     low = lax.broadcasted_iota(jnp.int32, (1, 128), 1) < CAP
     scale = 0.5 * HW ** (-0.5)
 
-    def attend(j, carry):
+    def project(b):
         for i in range(PER):
-            if i == 0:
-                @pl.when(j != SELF_BATCH)
+            rows_in, tags_in = arrival(b * PER + i)
+            if i == SELF_PLACE:
+                @pl.when(b != core)
                 def _():
-                    row_copy(j, 0).wait_recv()
-                    tag_copy(j, 0).wait_recv()
-
-                @pl.when(j == SELF_BATCH)
+                    rows_in.wait_recv()
+                    tags_in.wait_recv()
+
+                @pl.when(b == core)
                 def _():
                     self_copy.wait()
                     self_tag.wait()
             else:
-                row_copy(j, i).wait_recv()
-                tag_copy(j, i).wait_recv()
+                rows_in.wait_recv()
+                tags_in.wait_recv()
         tags = jnp.concatenate(
             [
-                jnp.where(low, tag_recv[j * PER], tag_recv[j * PER + 1]),
-                jnp.where(low, tag_recv[j * PER + 2], tag_recv[j * PER + 3]),
+                jnp.where(low, tag_recv[b * PER], tag_recv[b * PER + 1]),
+                jnp.where(low, tag_recv[b * PER + 2], tag_recv[b * PER + 3]),
             ],
             axis=1,
         )
         mask[...] = (user_mat[...] == tags).astype(jnp.float32)
-        rows = pl.ds(pl.multiple_of(j * BATCH, BATCH), BATCH)
-
-        def heads(step, carry):
-            for sub in range(HEAD_UNROLL):
-                h = step * HEAD_UNROLL + sub
-                kv = silu_half(
-                    0.5 * jnp.dot(recv[rows, :], kv_w[h], preferred_element_type=jnp.float32)
-                ).astype(jnp.bfloat16)
-                q_head = q_all[:, pl.ds(pl.multiple_of(h * HW, HW), HW)]
-                half = scale * lax.dot_general(
-                    q_head, kv[:, :HW], (((1,), (1,)), ((), ())),
-                    preferred_element_type=jnp.float32,
-                )
-                weight = (silu_half(half) * mask[...]).astype(jnp.bfloat16)
-                total[h] += jnp.dot(weight, kv[:, HW:], preferred_element_type=jnp.float32)
-            return carry
-
-        return lax.fori_loop(0, HEADS // HEAD_UNROLL, heads, carry)
-
-    lax.fori_loop(0, BATCHES, attend, 0)
-
+        rows = pl.ds(pl.multiple_of(b * BATCH, BATCH), BATCH)
+        for h in range(HEADS):
+            kv_ref[h] = silu_half(
+                0.5 * jnp.dot(recv[rows, :], kv_w[h], preferred_element_type=jnp.float32)
+            ).astype(jnp.bfloat16)
+
+    def attend_head(h):
+        half = scale * lax.dot_general(
+            q_all[:, h * HW : (h + 1) * HW], kv_ref[h, :, :HW], (((1,), (1,)), ((), ())),
+            preferred_element_type=jnp.float32,
+        )
+        weight = (silu_half(half) * mask[...]).astype(jnp.bfloat16)
+        return total[h] + jnp.dot(weight, kv_ref[h, :, HW:], preferred_element_type=jnp.float32)
+
+    def batch(b, carry):
+        project(b)
+
+        @pl.when(b == 0)
+        def _():
+            for d in range(1, SEQ):
+                q_copy(d).wait_recv()
+
+        for h in range(HEADS):
+            total[h] = attend_head(h)
+        return carry
+
+    lax.fori_loop(0, BATCHES - 1, batch, 0)
+    shift = total[0]
+    for h in range(1, HEADS):
+        shift = shift + total[h]
+    shift = jnp.sum(shift, axis=1, keepdims=True) * (1.0 / D)
     for h in range(HEADS):
-        part_send[:, h * HW : (h + 1) * HW] = total[h].astype(jnp.bfloat16)
+        total[h] = total[h] - shift
+    project(BATCHES - 1)
+    for h in range(HEADS):
+        head_total = attend_head(h)
+        total[h] = head_total
+        part_send[:, h * HW : (h + 1) * HW] = head_total.astype(jnp.bfloat16)
 
     def part_copy(d):
         peer = lax.rem(z + d, SEQ)
@@ -302,11 +336,11 @@
 
     def drain(j, carry):
         for i in range(PER):
-            if i == 0:
-                @pl.when(j != SELF_BATCH)
+            if i == SELF_PLACE:
+                @pl.when(j != self_part)
                 def _():
-                    row_copy(j, 0).wait_send()
-                    tag_copy(j, 0).wait_send()
+                    row_copy(j, i).wait_send()
+                    tag_copy(j, i).wait_send()
             else:
                 row_copy(j, i).wait_send()
                 tag_copy(j, i).wait_send()
@@ -342,10 +376,11 @@
             pltpu.VMEM((GROUP_CAND, D), bf16),
             pltpu.VMEM((GROUP_CAND, BATCH), f32),
             pltpu.VMEM((GROUP_CAND, BATCH), f32),
+            pltpu.VMEM((HEADS, BATCH, 2 * HW), bf16),
             pltpu.VMEM((HEADS, GROUP_CAND, HW), f32),
             pltpu.VMEM((GROUP_CAND, D), bf16),
             pltpu.VMEM((SEQ, CAND, D), bf16),
-            dma((3,)),
+            dma((6,)),
             dma((2 * HEADS,)),
             dma((GROUPS,)),
             dma((GROUPS,)),

time: 94.6 us -> 80.3 us (0.85)
  Pallas kernels: 92.9 us -> 78.6 us
    pallas_call x1, Pallas kernels: 92.9 us -> 78.6 us  [on_device(): pl.pallas_call(kernel, out_shape=jax.ShapeDtypeStruct((CAND, D), f32), in...]
where the time goes in v2:
time: 80.3 us; the launch traced here: 80.2 us
  Pallas kernels  78.6 us (98%)
  local copies, waits for them, and re-layouts  1.57 us (2%)
    pallas_call x1, Pallas kernels, on_device(): pl.pallas_call(kernel, out_shape=jax.ShapeDtypeStruct((CAND, D), f32), in...  78.6 us

profile of v2, /device:TPU:1, one launch (start us, length us, event | category | flops | bytes accessed | tf_op | source)
XLA Modules:
  0.0 80.2 jit_solution(14890305186168707057)
XLA Ops:
  0.0 78.6 %route_attend_score.1 = f32[32,1024]{1,0:T(8,128)} custom-call(bf16[1024,1024]{1,0:T(8,128)(2,1)} %history.1, s32[1,1024]{1,0:T(1,128)} %bitcast.3, s32[1,1024]{1,0:T(1,128)} %bitcast.4, bf16[32,1024]{1,0:T(8,128)(2,1)} %candidates.1, s32[1,256]{1,0:T(1,128)} %bitcast.5, bf16[1024,2048]{1,0:T(8,128)(2,1)} %w_qu.1, bf16[1024,2048]{1,0:T(8,128)(2,1)} %w_kv.1, ...), custom_call_target="tpu_custom_call" | custom-call | tf_op jit(solution)/shard_map/route_attend_score/pallas_call | solution.py:360
  78.6 1.6 %copy.10 = f32[32,1024]{1,0:T(8,128)} copy(f32[32,1024]{1,0:T(8,128)} %route_attend_score.1) | data formatting | bytes 262144

commit v3 on v2

--- a/solution.py
+++ b/solution.py
@@ -21,7 +21,11 @@
 BATCHES = GROUPS // PER
 MESH = pl.DeviceIdType.MESH
 PACKED_FIRST = 2
+SELF_TURN = 1
 SELF_PLACE = 3
+LAST = 2 * BATCH
+SLICE = 2
+SLICES = HEADS // SLICE
 
 
 def silu_half(half):
@@ -108,11 +112,11 @@
 
     def target(j, i):
         jj = lax.rem(j, 4)
-        a = jnp.where(jj == 2, 2, 1)
+        a = jnp.where(jj == 0, 2, 1)
         b = jnp.where(jj == 3, 0, 1)
         dx, dy = ((a, b), (-b, a), (-a, -b), (b, -a))[i]
-        dx = jnp.where(jj == 0, 2 * (1 - i % 2), dx)
-        dy = jnp.where(jj == 0, 2 * (1 - i // 2), dy)
+        dx = jnp.where(jj == SELF_TURN, 2 * (1 - i % 2), dx)
+        dy = jnp.where(jj == SELF_TURN, 2 * (1 - i // 2), dy)
         to_x = lax.rem(x + sign * dx + 4, 4)
         to_y = lax.rem(y + sign * dy + 4, 4)
         return to_x * 8 + to_y * 2 + lax.div(j, 4)
@@ -148,13 +152,14 @@
             ),
         )
 
-    self_part = core * 4
+    self_part = core * 4 + SELF_TURN
+    self_batch = 2 * SELF_TURN + core
     self_copy = pltpu.make_async_copy(
-        send.at[block(self_part * PER + SELF_PLACE)], recv.at[block(core * PER + SELF_PLACE)],
+        send.at[block(self_part * PER + SELF_PLACE)], recv.at[block(self_batch * PER + SELF_PLACE)],
         self_sem.at[0],
     )
     self_tag = pltpu.make_async_copy(
-        tag_send.at[2 * self_part + SELF_PLACE // 2], tag_recv.at[core * PER + SELF_PLACE],
+        tag_send.at[2 * self_part + SELF_PLACE // 2], tag_recv.at[self_batch * PER + SELF_PLACE],
         self_sem.at[1],
     )
 
@@ -245,16 +250,16 @@
     low = lax.broadcasted_iota(jnp.int32, (1, 128), 1) < CAP
     scale = 0.5 * HW ** (-0.5)
 
-    def project(b):
+    def take_in(b, half):
         for i in range(PER):
             rows_in, tags_in = arrival(b * PER + i)
             if i == SELF_PLACE:
-                @pl.when(b != core)
+                @pl.when(b != self_batch)
                 def _():
                     rows_in.wait_recv()
                     tags_in.wait_recv()
 
-                @pl.when(b == core)
+                @pl.when(b == self_batch)
                 def _():
                     self_copy.wait()
                     self_tag.wait()
@@ -268,23 +273,28 @@
             ],
             axis=1,
         )
-        mask[...] = (user_mat[...] == tags).astype(jnp.float32)
-        rows = pl.ds(pl.multiple_of(b * BATCH, BATCH), BATCH)
+        mask[:, half * BATCH : (half + 1) * BATCH] = (user_mat[...] == tags).astype(jnp.float32)
+
+    def project_head(h, first, count):
+        rows = pl.ds(pl.multiple_of(first, BATCH), count)
+        kv_ref[h, :count] = silu_half(
+            0.5 * jnp.dot(recv[rows, :], kv_w[h], preferred_element_type=jnp.float32)
+        ).astype(jnp.bfloat16)
+
+    def attend_head(h, count):
+        half = scale * lax.dot_general(
+            q_all[:, h * HW : (h + 1) * HW], kv_ref[h, :count, :HW], (((1,), (1,)), ((), ())),
+            preferred_element_type=jnp.float32,
+        )
+        weight = (silu_half(half) * mask[:, :count]).astype(jnp.bfloat16)
+        return total[h] + jnp.dot(
+            weight, kv_ref[h, :count, HW:], preferred_element_type=jnp.float32
+        )
+
+    def batch(b, carry):
+        take_in(b, 0)
         for h in range(HEADS):
-            kv_ref[h] = silu_half(
-                0.5 * jnp.dot(recv[rows, :], kv_w[h], preferred_element_type=jnp.float32)
-            ).astype(jnp.bfloat16)
-
-    def attend_head(h):
-        half = scale * lax.dot_general(
-            q_all[:, h * HW : (h + 1) * HW], kv_ref[h, :, :HW], (((1,), (1,)), ((), ())),
-            preferred_element_type=jnp.float32,
-        )
-        weight = (silu_half(half) * mask[...]).astype(jnp.bfloat16)
-        return total[h] + jnp.dot(weight, kv_ref[h, :, HW:], preferred_element_type=jnp.float32)
-
-    def batch(b, carry):
-        project(b)
+            project_head(h, b * BATCH, BATCH)
 
         @pl.when(b == 0)
         def _():
@@ -292,37 +302,50 @@
                 q_copy(d).wait_recv()
 
         for h in range(HEADS):
-            total[h] = attend_head(h)
+            total[h] = attend_head(h, BATCH)
         return carry
 
-    lax.fori_loop(0, BATCHES - 1, batch, 0)
+    lax.fori_loop(0, BATCHES - 2, batch, 0)
     shift = total[0]
     for h in range(1, HEADS):
         shift = shift + total[h]
     shift = jnp.sum(shift, axis=1, keepdims=True) * (1.0 / D)
     for h in range(HEADS):
         total[h] = total[h] - shift
-    project(BATCHES - 1)
-    for h in range(HEADS):
-        head_total = attend_head(h)
-        total[h] = head_total
-        part_send[:, h * HW : (h + 1) * HW] = head_total.astype(jnp.bfloat16)
-
-    def part_copy(d):
+
+    def part_copy(d, n):
         peer = lax.rem(z + d, SEQ)
+        cols = pl.ds(n * SLICE * HW, SLICE * HW)
         return pltpu.make_async_remote_copy(
-            part_send.at[pl.ds(pl.multiple_of(peer * CAND, CAND), CAND)],
-            part_recv.at[d], part_send_sem.at[d], part_recv_sem.at[d],
+            part_send.at[pl.ds(pl.multiple_of(peer * CAND, CAND), CAND), cols],
+            part_recv.at[d, :, cols],
+            part_send_sem.at[n * SEQ + d], part_recv_sem.at[n * SEQ + d],
             device_id=(dp, peer), device_id_type=MESH,
         )
 
-    for d in (4, 3, 5, 2, 6, 1, 7):
-        part_copy(d).start()
+    take_in(BATCHES - 2, 0)
+    take_in(BATCHES - 1, 1)
+    for n in range(SLICES + 1):
+        for h in range(n * SLICE, min((n + 1) * SLICE, HEADS)):
+            project_head(h, GROUPS * CAP - LAST, LAST)
+        if n:
+            for h in range((n - 1) * SLICE, n * SLICE):
+                head_total = attend_head(h, LAST)
+                total[h] = head_total
+                part_send[:, h * HW : (h + 1) * HW] = head_total.astype(jnp.bfloat16)
+            for d in (4, 3, 5, 2, 6, 1, 7):
+                part_copy(d, n - 1).start()
+
     load_out.wait()
-    attended = jnp.concatenate([total[h, own_rows, :] for h in range(HEADS)], axis=1)
-    for d in (1, 7, 2, 6, 3, 5, 4):
-        part_copy(d).wait_recv()
-        attended = attended + part_recv[d].astype(jnp.float32)
+    slices = []
+    for n in range(SLICES):
+        heads = range(n * SLICE, (n + 1) * SLICE)
+        some = jnp.concatenate([total[h, own_rows, :] for h in heads], axis=1)
+        for d in (1, 7, 2, 6, 3, 5, 4):
+            part_copy(d, n).wait_recv()
+            some = some + part_recv[d, :, n * SLICE * HW : (n + 1) * SLICE * HW].astype(jnp.float32)
+        slices.append(some)
+    attended = jnp.concatenate(slices, axis=1)
     mean = jnp.mean(attended, axis=1, keepdims=True)
     centered = attended - mean
     variance = jnp.mean(centered * centered, axis=1, keepdims=True)
@@ -349,7 +372,8 @@
     lax.fori_loop(0, BATCHES, drain, 0)
     for d in range(1, SEQ):
         q_copy(d).wait_send()
-        part_copy(d).wait_send()
+        for n in range(SLICES):
+            part_copy(d, n).wait_send()
 
 
 def on_device(history, hist_dest, hist_user, candidates, cand_user, w_qu, w_kv, w_out):
@@ -375,8 +399,8 @@
             pltpu.VMEM((CAND, 2 * D), bf16),
             pltpu.VMEM((GROUP_CAND, D), bf16),
             pltpu.VMEM((GROUP_CAND, BATCH), f32),
-            pltpu.VMEM((GROUP_CAND, BATCH), f32),
-            pltpu.VMEM((HEADS, BATCH, 2 * HW), bf16),
+            pltpu.VMEM((GROUP_CAND, LAST), f32),
+            pltpu.VMEM((HEADS, LAST, 2 * HW), bf16),
             pltpu.VMEM((HEADS, GROUP_CAND, HW), f32),
             pltpu.VMEM((GROUP_CAND, D), bf16),
             pltpu.VMEM((SEQ, CAND, D), bf16),
@@ -388,8 +412,8 @@
             dma((GROUPS,)),
             dma((SEQ,)),
             dma((SEQ,)),
-            dma((SEQ,)),
-            dma((SEQ,)),
+            dma((SEQ * SLICES,)),
+            dma((SEQ * SLICES,)),
             dma((2,)),
         ],
         compiler_params=pltpu.CompilerParams(

time: 80.3 us -> 83 us (1.034)
  Pallas kernels: 78.6 us -> 81.3 us
    pallas_call x1, Pallas kernels: 78.6 us -> 81.3 us  [on_device(): pl.pallas_call(kernel, out_shape=jax.ShapeDtypeStruct((CAND, D), f32), in...]
where the time goes in v3:
time: 83 us; the launch traced here: 82.8 us
  Pallas kernels  81.3 us (98%)
  local copies, waits for them, and re-layouts  1.57 us (2%)
    pallas_call x1, Pallas kernels, on_device(): pl.pallas_call(kernel, out_shape=jax.ShapeDtypeStruct((CAND, D), f32), in...  81.3 us

profile of v3, /device:TPU:1, one launch (start us, length us, event | category | flops | bytes accessed | tf_op | source)
XLA Modules:
  0.0 82.8 jit_solution(14565413463803353191)
XLA Ops:
  0.0 81.3 %route_attend_score.1 = f32[32,1024]{1,0:T(8,128)} custom-call(bf16[1024,1024]{1,0:T(8,128)(2,1)} %history.1, s32[1,1024]{1,0:T(1,128)} %bitcast.3, s32[1,1024]{1,0:T(1,128)} %bitcast.4, bf16[32,1024]{1,0:T(8,128)(2,1)} %candidates.1, s32[1,256]{1,0:T(1,128)} %bitcast.5, bf16[1024,2048]{1,0:T(8,128)(2,1)} %w_qu.1, bf16[1024,2048]{1,0:T(8,128)(2,1)} %w_kv.1, ...), custom_call_target="tpu_custom_call" | custom-call | tf_op jit(solution)/shard_map/route_attend_score/pallas_call | solution.py:384
  81.3 1.6 %copy.10 = f32[32,1024]{1,0:T(8,128)} copy(f32[32,1024]{1,0:T(8,128)} %route_attend_score.1) | data formatting | bytes 262144

commit v4 on v3

--- a/solution.py
+++ b/solution.py
@@ -21,7 +21,6 @@
 BATCHES = GROUPS // PER
 MESH = pl.DeviceIdType.MESH
 PACKED_FIRST = 2
-SELF_TURN = 1
 SELF_PLACE = 3
 LAST = 2 * BATCH
 SLICE = 2
@@ -112,11 +111,11 @@
 
     def target(j, i):
         jj = lax.rem(j, 4)
-        a = jnp.where(jj == 0, 2, 1)
+        a = jnp.where(jj == 2, 2, 1)
         b = jnp.where(jj == 3, 0, 1)
         dx, dy = ((a, b), (-b, a), (-a, -b), (b, -a))[i]
-        dx = jnp.where(jj == SELF_TURN, 2 * (1 - i % 2), dx)
-        dy = jnp.where(jj == SELF_TURN, 2 * (1 - i // 2), dy)
+        dx = jnp.where(jj == 0, 2 * (1 - i % 2), dx)
+        dy = jnp.where(jj == 0, 2 * (1 - i // 2), dy)
         to_x = lax.rem(x + sign * dx + 4, 4)
         to_y = lax.rem(y + sign * dy + 4, 4)
         return to_x * 8 + to_y * 2 + lax.div(j, 4)
@@ -152,14 +151,13 @@
             ),
         )
 
-    self_part = core * 4 + SELF_TURN
-    self_batch = 2 * SELF_TURN + core
+    self_part = core * 4
     self_copy = pltpu.make_async_copy(
-        send.at[block(self_part * PER + SELF_PLACE)], recv.at[block(self_batch * PER + SELF_PLACE)],
+        send.at[block(self_part * PER + SELF_PLACE)], recv.at[block(core * PER + SELF_PLACE)],
         self_sem.at[0],
     )
     self_tag = pltpu.make_async_copy(
-        tag_send.at[2 * self_part + SELF_PLACE // 2], tag_recv.at[self_batch * PER + SELF_PLACE],
+        tag_send.at[2 * self_part + SELF_PLACE // 2], tag_recv.at[core * PER + SELF_PLACE],
         self_sem.at[1],
     )
 
@@ -254,12 +252,12 @@
         for i in range(PER):
             rows_in, tags_in = arrival(b * PER + i)
             if i == SELF_PLACE:
-                @pl.when(b != self_batch)
+                @pl.when(b != core)
                 def _():
                     rows_in.wait_recv()
                     tags_in.wait_recv()
 
-                @pl.when(b == self_batch)
+                @pl.when(b == core)
                 def _():
                     self_copy.wait()
                     self_tag.wait()

time: 83 us -> 78.8 us (0.949)
  Pallas kernels: 81.3 us -> 77.1 us
    pallas_call x1, Pallas kernels: 81.3 us -> 77.1 us  [on_device(): pl.pallas_call(kernel, out_shape=jax.ShapeDtypeStruct((CAND, D), f32), in...]
where the time goes in v4:
time: 78.8 us; the launch traced here: 78.6 us
  Pallas kernels  77.1 us (98%)
  local copies, waits for them, and re-layouts  1.57 us (2%)
    pallas_call x1, Pallas kernels, on_device(): pl.pallas_call(kernel, out_shape=jax.ShapeDtypeStruct((CAND, D), f32), in...  77.1 us

profile of v4, /device:TPU:1, one launch (start us, length us, event | category | flops | bytes accessed | tf_op | source)
XLA Modules:
  0.0 78.6 jit_solution(6685795331267366144)
XLA Ops:
  0.0 77.1 %route_attend_score.1 = f32[32,1024]{1,0:T(8,128)} custom-call(bf16[1024,1024]{1,0:T(8,128)(2,1)} %history.1, s32[1,1024]{1,0:T(1,128)} %bitcast.3, s32[1,1024]{1,0:T(1,128)} %bitcast.4, bf16[32,1024]{1,0:T(8,128)(2,1)} %candidates.1, s32[1,256]{1,0:T(1,128)} %bitcast.5, bf16[1024,2048]{1,0:T(8,128)(2,1)} %w_qu.1, bf16[1024,2048]{1,0:T(8,128)(2,1)} %w_kv.1, ...), custom_call_target="tpu_custom_call" | custom-call | tf_op jit(solution)/shard_map/route_attend_score/pallas_call | solution.py:382
  77.1 1.6 %copy.10 = f32[32,1024]{1,0:T(8,128)} copy(f32[32,1024]{1,0:T(8,128)} %route_attend_score.1) | data formatting | bytes 262144

commit v5 on v4

--- a/solution.py
+++ b/solution.py
@@ -112,7 +112,7 @@
     def target(j, i):
         jj = lax.rem(j, 4)
         a = jnp.where(jj == 2, 2, 1)
-        b = jnp.where(jj == 3, 0, 1)
+        b = jnp.where(jj == 1, 0, 1)
         dx, dy = ((a, b), (-b, a), (-a, -b), (b, -a))[i]
         dx = jnp.where(jj == 0, 2 * (1 - i % 2), dx)
         dy = jnp.where(jj == 0, 2 * (1 - i // 2), dy)

time: 78.8 us -> 78.9 us (level)
  no operation moved by 1% of the time
where the time goes in v5:
time: 78.9 us; the launch traced here: 78.7 us
  Pallas kernels  77.2 us (98%)
  local copies, waits for them, and re-layouts  1.57 us (2%)
    pallas_call x1, Pallas kernels, on_device(): pl.pallas_call(kernel, out_shape=jax.ShapeDtypeStruct((CAND, D), f32), in...  77.2 us

profile of v5, /device:TPU:1, one launch (start us, length us, event | category | flops | bytes accessed | tf_op | source)
XLA Modules:
  0.0 78.7 jit_solution(15330820050329724987)
XLA Ops:
  0.0 77.2 %route_attend_score.1 = f32[32,1024]{1,0:T(8,128)} custom-call(bf16[1024,1024]{1,0:T(8,128)(2,1)} %history.1, s32[1,1024]{1,0:T(1,128)} %bitcast.3, s32[1,1024]{1,0:T(1,128)} %bitcast.4, bf16[32,1024]{1,0:T(8,128)(2,1)} %candidates.1, s32[1,256]{1,0:T(1,128)} %bitcast.5, bf16[1024,2048]{1,0:T(8,128)(2,1)} %w_qu.1, bf16[1024,2048]{1,0:T(8,128)(2,1)} %w_kv.1, ...), custom_call_target="tpu_custom_call" | custom-call | tf_op jit(solution)/shard_map/route_attend_score/pallas_call | solution.py:382
  77.2 1.6 %copy.10 = f32[32,1024]{1,0:T(8,128)} copy(f32[32,1024]{1,0:T(8,128)} %route_attend_score.1) | data formatting | bytes 262144

commit v6 on v5

--- a/solution.py
+++ b/solution.py
@@ -111,8 +111,8 @@
 
     def target(j, i):
         jj = lax.rem(j, 4)
-        a = jnp.where(jj == 2, 2, 1)
-        b = jnp.where(jj == 1, 0, 1)
+        a = jnp.where((j == 2) | (j == 5), 2, 1)
+        b = jnp.where((j == 3) | (j == 6), 0, 1)
         dx, dy = ((a, b), (-b, a), (-a, -b), (b, -a))[i]
         dx = jnp.where(jj == 0, 2 * (1 - i % 2), dx)
         dy = jnp.where(jj == 0, 2 * (1 - i // 2), dy)

time: 78.9 us -> 77.4 us (0.981)
  Pallas kernels: 77.2 us -> 75.6 us
    pallas_call x1, Pallas kernels: 77.2 us -> 75.6 us  [on_device(): pl.pallas_call(kernel, out_shape=jax.ShapeDtypeStruct((CAND, D), f32), in...]
where the time goes in v6:
time: 77.4 us; the launch traced here: 77.2 us
  Pallas kernels  75.6 us (98%)
  local copies, waits for them, and re-layouts  1.57 us (2%)
    pallas_call x1, Pallas kernels, on_device(): pl.pallas_call(kernel, out_shape=jax.ShapeDtypeStruct((CAND, D), f32), in...  75.6 us
    unnamed x1, local copies, waits for them, and re-layouts  1.57 us

profile of v6, /device:TPU:1, one launch (start us, length us, event | category | flops | bytes accessed | tf_op | source)
XLA Modules:
  0.0 77.2 jit_solution(9484008207381672688)
XLA Ops:
  0.0 75.6 %route_attend_score.1 = f32[32,1024]{1,0:T(8,128)} custom-call(bf16[1024,1024]{1,0:T(8,128)(2,1)} %history.1, s32[1,1024]{1,0:T(1,128)} %bitcast.3, s32[1,1024]{1,0:T(1,128)} %bitcast.4, bf16[32,1024]{1,0:T(8,128)(2,1)} %candidates.1, s32[1,256]{1,0:T(1,128)} %bitcast.5, bf16[1024,2048]{1,0:T(8,128)(2,1)} %w_qu.1, bf16[1024,2048]{1,0:T(8,128)(2,1)} %w_kv.1, ...), custom_call_target="tpu_custom_call" | custom-call | tf_op jit(solution)/shard_map/route_attend_score/pallas_call | solution.py:382
  75.6 1.6 %copy.10 = f32[32,1024]{1,0:T(8,128)} copy(f32[32,1024]{1,0:T(8,128)} %route_attend_score.1) | data formatting | bytes 262144

commit v7 on v6

--- a/solution.py
+++ b/solution.py
@@ -22,6 +22,7 @@
 MESH = pl.DeviceIdType.MESH
 PACKED_FIRST = 2
 SELF_PLACE = 3
+ORDER = (0, 1, 4, 2, 3, 5, 6, 7)
 LAST = 2 * BATCH
 SLICE = 2
 SLICES = HEADS // SLICE
@@ -201,12 +202,18 @@
                 row_copy(j, i).start()
                 tag_copy(j, i).start()
 
+    def part_at(place):
+        part = place
+        for at, value in enumerate(ORDER):
+            part = jnp.where(place == at, value, part)
+        return part
+
     def dispatch_and_pack(j, carry):
-        dispatch(j)
-        pack(j + 1)
+        dispatch(part_at(j))
+        pack(part_at(j + 1))
         return carry
 
-    pack(0)
+    pack(ORDER[0])
     pl.semaphore_wait(barrier, GROUPS - 1 + SEQ - 1)
     lax.fori_loop(0, PACKED_FIRST, dispatch_and_pack, 0)
 
@@ -229,7 +236,7 @@
     for d in range(1, SEQ):
         q_copy(d).start()
     lax.fori_loop(PACKED_FIRST, BATCHES - 1, dispatch_and_pack, 0)
-    dispatch(BATCHES - 1)
+    dispatch(ORDER[-1])
 
     square = (
         lax.broadcasted_iota(jnp.int32, (GROUP_CAND, GROUP_CAND), 0)

time: 77.4 us -> 77.5 us (level)
  no operation moved by 1% of the time
where the time goes in v7:
time: 77.5 us; the launch traced here: 77.3 us
  Pallas kernels  75.7 us (98%)
  local copies, waits for them, and re-layouts  1.57 us (2%)
    pallas_call x1, Pallas kernels, on_device(): pl.pallas_call(kernel, out_shape=jax.ShapeDtypeStruct((CAND, D), f32), in...  75.7 us
    unnamed x1, local copies, waits for them, and re-layouts  1.57 us

profile of v7, /device:TPU:1, one launch (start us, length us, event | category | flops | bytes accessed | tf_op | source)
XLA Modules:
  0.0 77.3 jit_solution(2521191691716642932)
XLA Ops:
  0.0 75.7 %route_attend_score.1 = f32[32,1024]{1,0:T(8,128)} custom-call(bf16[1024,1024]{1,0:T(8,128)(2,1)} %history.1, s32[1,1024]{1,0:T(1,128)} %bitcast.3, s32[1,1024]{1,0:T(1,128)} %bitcast.4, bf16[32,1024]{1,0:T(8,128)(2,1)} %candidates.1, s32[1,256]{1,0:T(1,128)} %bitcast.5, bf16[1024,2048]{1,0:T(8,128)(2,1)} %w_qu.1, bf16[1024,2048]{1,0:T(8,128)(2,1)} %w_kv.1, ...), custom_call_target="tpu_custom_call" | custom-call | tf_op jit(solution)/shard_map/route_attend_score/pallas_call | solution.py:389
  75.7 1.6 %copy.10 = f32[32,1024]{1,0:T(8,128)} copy(f32[32,1024]{1,0:T(8,128)} %route_attend_score.1) | data formatting | bytes 262144
